TPU v7x, 256 devices: a whole 4x4x8 slice. The times are simulated.
256 devices in a mesh: dp: 32 (over y, z_hi, x), seq: 8 (over z_lo, core).
Axes of the slice: x: 4, y: 4, z: 8 (z_hi: 2, z_lo: 4; z = z_hi * 4 + z_lo), core: 2. Of those that a mesh axis runs over, the one named last changes fastest.
Arguments:
- prompt_hidden: bfloat16 [32, 2048, 5120], P('dp', 'seq'), may hold values from -6 to 6
- key_value_weight: bfloat16 [5120, 2048], P(('dp', 'seq')), may hold values from -0.078125 to 0.078125
- key_norm_gain: float32 [1024], replicated, may hold values from 0.25 to 1.75
- page_table: int32 [32, 16], replicated, may hold values from 0 to 15, each once within a row
- lengths: int32 [32], replicated, may hold values from 512 to 2048, as said below
- source_replica: int32 [32], replicated, may hold values from 0 to 31, as said below
- decode_hidden: bfloat16 [3, 512, 5120], P(None, 'dp'), may hold values from -6 to 6
- queries: bfloat16 [3, 512, 5120], P(None, 'dp', 'seq'), may hold values from -1 to 1
Outputs:
- attended: bfloat16 [3, 512, 5120], P(None, 'dp', 'seq')
- forked_cache: float32 [32, 2, 2048, 1024], P('dp', None, None, 'seq')
Inputs may be any that keep to these rules, and one draw needn't show every extreme that they name: `lengths`: some prompt has exactly 2048 tokens and some exactly 512. source_replica[r] is r XOR one nonzero number that is the same for all replicas.
All inputs are finite; a program needn't handle non-finite values.
Results may differ from a plain program's by a relative error of at most 0.0059.
Values may be sent and summed in bfloat16 or wider, within the bound.
A program may use at most 128 MiB of HBM per device.

v0:
```python
import math

import jax
import jax.numpy as jnp
from jax import lax
from jax.sharding import PartitionSpec as P

KEY_VALUE_HEADS = 8
HEAD_SIZE = 128
PAGE_TOKENS = 128
QUERY_PER_KV = 5


def swapped_2(array, axis, distance):
    return lax.ppermute(array, axis, [(i, i ^ 1 << distance) for i in range(lax.axis_size(axis))])


def page_positions(table):
    return (
        table[:, None] * PAGE_TOKENS + jnp.arange(PAGE_TOKENS, dtype=jnp.int32)[None, :]
    ).reshape(-1)


def root_mean_keys(raw_keys, norm_gain):
    return (
        raw_keys
        * lax.rsqrt(jnp.mean(raw_keys * raw_keys, axis=-1, keepdims=True) + 1e-06)
        * norm_gain
    )


def rotate(head_split, places):
    half = head_split.shape[-1] // 2
    freq = 500000.0 ** (-jnp.arange(half, dtype=jnp.float32) * 2.0 / head_split.shape[-1])
    angle = places.astype(jnp.float32)[..., None, None] * freq
    cosine = jnp.cos(angle)
    sine = jnp.sin(angle)
    first = head_split[..., :half]
    second = head_split[..., half:]
    return jnp.concatenate(
        [first * cosine - second * sine, second * cosine + first * sine], axis=-1
    )


def prepare(projected_rows, norm_gain, places, length):
    key_width = KEY_VALUE_HEADS * HEAD_SIZE
    key_rows = root_mean_keys(projected_rows[:, :key_width], norm_gain).reshape(
        -1, KEY_VALUE_HEADS, HEAD_SIZE
    )
    key_rows = rotate(key_rows, places).reshape(-1, key_width)
    values = projected_rows[:, key_width:]
    live = (places < length)[None, :, None]
    return jnp.where(live, jnp.stack([key_rows, values]), jnp.float32(0.0))


def quantize(cache_fields):
    token_count = cache_fields.shape[1]
    paged_cache = cache_fields.reshape(
        2, token_count // PAGE_TOKENS, PAGE_TOKENS, KEY_VALUE_HEADS, HEAD_SIZE
    )
    largest = jnp.max(jnp.abs(paged_cache), axis=(2, 4))
    inverse_scale = ((largest + 1e-06) / 448.0).astype(jnp.bfloat16)
    stored_pages = (paged_cache / inverse_scale[:, :, None, :, None].astype(jnp.float32)).astype(
        jnp.bfloat16
    )
    return (stored_pages.reshape(2, token_count, KEY_VALUE_HEADS * HEAD_SIZE), inverse_scale)


def expand(pool, inverse_scale):
    token_count = pool.shape[1]
    head_split = inverse_scale.shape[2]
    paged_cache = pool.reshape(
        2, token_count // PAGE_TOKENS, PAGE_TOKENS, head_split, HEAD_SIZE
    ).astype(jnp.float32)
    return (paged_cache * inverse_scale[:, :, None, :, None].astype(jnp.float32)).reshape(
        2, token_count, head_split * HEAD_SIZE
    )


def attend(head_split, pool, inverse_scale, places, length, fresh_key_rows, fresh_value_rows):
    steps = head_split.shape[0]
    groups = head_split.shape[2]
    key_rows = pool[0].reshape(-1, groups, HEAD_SIZE)
    values = pool[1].reshape(-1, groups, HEAD_SIZE)
    factor = 1.0 / math.sqrt(HEAD_SIZE)
    key_scale = jnp.repeat(inverse_scale[0].astype(jnp.float32), PAGE_TOKENS, axis=0).T
    value_scale = jnp.repeat(inverse_scale[1].astype(jnp.float32), PAGE_TOKENS, axis=0).T
    raw = jnp.einsum("sijgd,tjd->sijgt", head_split, key_rows, preferred_element_type=jnp.float32)
    cached = jnp.where(
        places < length, jnp.exp(raw * key_scale[None, None, :, None, :] * factor), jnp.float32(0.0)
    )
    fresh_raw = jnp.einsum(
        "sijgd,uijd->sijgu", head_split, fresh_key_rows, preferred_element_type=jnp.float32
    )
    visible = jnp.arange(steps)[:, None] >= jnp.arange(steps)[None, :]
    fresh = jnp.where(
        visible[:, None, None, None, :], jnp.exp(fresh_raw * factor), jnp.float32(0.0)
    )
    total = jnp.sum(cached, axis=-1) + jnp.sum(fresh, axis=-1)
    cached_weight = (cached / total[..., None] * value_scale[None, None, :, None, :]).astype(
        jnp.bfloat16
    )
    fresh_weight = (fresh / total[..., None]).astype(jnp.bfloat16)
    result = jnp.einsum(
        "sijgt,tjd->sijgd", cached_weight, values, preferred_element_type=jnp.float32
    )
    return result + jnp.einsum(
        "sijgu,uijd->sijgd", fresh_weight, fresh_value_rows, preferred_element_type=jnp.float32
    )


def copy_pages(pool, inverse_scale, partner_mask, replicas):
    for bit in range(replicas.bit_length() - 1):
        swapped, swapped_scale = swapped_2((pool, inverse_scale), "dp", bit)
        taken = jnp.bitwise_and(jnp.right_shift(partner_mask, bit), 1) == 1
        pool = jnp.where(taken, swapped, pool)
        inverse_scale = jnp.where(taken, swapped_scale, inverse_scale)
    result = (pool, inverse_scale)
    return result


def on_device(
    prompt_hidden,
    key_value_weight,
    key_norm_gain,
    page_table,
    lengths,
    source_replica,
    decode_hidden,
    queries,
):
    steps, paired, width = queries.shape
    single = paired // 2
    replicas = lax.axis_size("dp")
    seq_at = lax.axis_index("seq")
    replica = lax.axis_index("dp")
    tok_here = prompt_hidden.shape[1]
    pages_here = tok_here // PAGE_TOKENS
    heads_here = width // (QUERY_PER_KV * HEAD_SIZE)
    decode_rows = decode_hidden.reshape(steps * paired, decode_hidden.shape[2])
    all_rows = jnp.concatenate([prompt_hidden[0], decode_rows], axis=0)
    projected_rows = jnp.dot(
        all_rows,
        lax.all_gather(key_value_weight, ("dp", "seq"), axis=0, tiled=True),
        preferred_element_type=jnp.float32,
    )
    table_here = lax.dynamic_slice(page_table, (replica, seq_at * pages_here), (1, pages_here))[0]
    own_length = lengths[replica]
    partner = source_replica[replica]
    partner_mask = jnp.bitwise_xor(partner, replica)
    far_length = lengths[partner]
    stored_pages, scales = quantize(
        prepare(projected_rows[:tok_here], key_norm_gain, page_positions(table_here), own_length)
    )
    pool, pool_scale = (
        lax.all_to_all(stored_pages, "seq", split_axis=2, concat_axis=1, tiled=True),
        lax.all_to_all(scales, "seq", split_axis=2, concat_axis=1, tiled=True),
    )
    far_pool, far_scale = copy_pages(pool, pool_scale, partner_mask, replicas)
    decode_portion = projected_rows[tok_here:].reshape(steps, paired, -1)
    offset = seq_at * heads_here * HEAD_SIZE
    gathered_keys = root_mean_keys(
        decode_portion[..., : KEY_VALUE_HEADS * HEAD_SIZE], key_norm_gain
    )
    fresh_key_rows = lax.dynamic_slice_in_dim(
        gathered_keys, offset, heads_here * HEAD_SIZE, 2
    ).reshape(steps, paired, heads_here, HEAD_SIZE)
    gathered_values = decode_portion[..., KEY_VALUE_HEADS * HEAD_SIZE :]
    fresh_value_rows = (
        lax.dynamic_slice_in_dim(gathered_values, offset, heads_here * HEAD_SIZE, 2)
        .reshape(steps, paired, heads_here, HEAD_SIZE)
        .astype(jnp.bfloat16)
    )
    starts = jnp.concatenate(
        [jnp.full((single,), own_length, jnp.int32), jnp.full((single,), far_length, jnp.int32)]
    )
    new_places = starts[None, :] + jnp.arange(steps, dtype=jnp.int32)[:, None]
    fresh_key_rows = rotate(fresh_key_rows, new_places).astype(jnp.bfloat16)
    head_split = queries.reshape(steps, paired, heads_here, QUERY_PER_KV, HEAD_SIZE)
    near = attend(
        head_split[:, :single],
        pool,
        pool_scale,
        page_positions(page_table[replica]),
        own_length,
        fresh_key_rows[:, :single],
        fresh_value_rows[:, :single],
    )
    far = attend(
        head_split[:, single:],
        far_pool,
        far_scale,
        page_positions(page_table[partner]),
        far_length,
        fresh_key_rows[:, single:],
        fresh_value_rows[:, single:],
    )
    attended = (
        jnp.concatenate([near, far], axis=1).reshape(steps, paired, width).astype(jnp.bfloat16)
    )
    forked_cache = expand(far_pool, far_scale)[None]
    return (attended, forked_cache)


def solution(mesh):
    return jax.shard_map(
        on_device,
        mesh=mesh,
        in_specs=(
            P("dp", "seq", None),
            P(("dp", "seq"), None),
            P(),
            P(),
            P(),
            P(),
            P(None, "dp", None),
            P(None, "dp", "seq"),
        ),
        out_specs=(P(None, "dp", "seq"), P("dp", None, None, "seq")),
        check_vma=False,
    )
```

profile of v0, /device:TPU:6, one launch (start us, length us, event | category | flops | bytes accessed | tf_op | source)
XLA Modules:
  0.0 703.6 jit_solution(15181870796804784816)
XLA Ops:
  15.4 434.9 %all-gather.3.cloned.1.call-done = bf16[256,20,2048]{2,1,0:T(8,128)(2,1)} async-done(((bf16[1,20,2048]{2,1,0:T(8,128)(2,1)}), bf16[256,20,2048]{2,1,0:T(8,128)(2,1)}) %all-gather.3.cloned.1.call-update) | async-done | bytes 20971536 | tf_op jit(solution)/shard_map/all_gather | solution.py:144
  450.3 31.5 %reshape.470 = bf16[5120,2048]{1,0:T(8,128)(2,1)} reshape(bf16[256,20,2048]{2,1,0:T(8,128)(2,1)} %all-gather.3.cloned.1.call-done) | data formatting | bytes 41943040
  481.8 11.5 %fusion = f32[304,2048]{1,0:T(8,128)S(1)} fusion(bf16[5120,2048]{1,0:T(8,128)(2,1)} %reshape.470, bf16[48,5120]{1,0:T(8,128)(2,1)S(1)} %bitcast.234, bf16[256,5120]{1,0:T(8,128)(2,1)} %bitcast.233), kind=kOutput, calls=%fused_computation | convolution fusion | flops 6381568000 | bytes 26574848 | tf_op jit(solution)/shard_map/dot_general | solution.py:142
  497.9 1.5 div.75
  499.4 1.7 div.76
  501.1 2.5 fusion.15
  503.6 3.7 copy.79
  507.3 7.5 %all-to-all-start = ((bf16[2,256,1024]{1,0,2:T(2,128)(2,1)}), bf16[2,256,1024]{1,0,2:T(2,128)(2,1)S(1)}, u32[]{:S(2)}, u32[]{:S(2)}) async-start(bf16[2,256,1024]{1,0,2:T(2,128)(2,1)} %copy.79), calls=%async_computation | async-start | bytes 2097152 | tf_op jit(solution)/shard_map/all_to_all | solution.py:156
  517.1 24.3 %all-to-all-done = bf16[2,256,1024]{1,0,2:T(2,128)(2,1)S(1)} async-done(((bf16[2,256,1024]{1,0,2:T(2,128)(2,1)}), bf16[2,256,1024]{1,0,2:T(2,128)(2,1)S(1)}, u32[]{:S(2)}, u32[]{:S(2)}) %all-to-all-start) | async-done | bytes 1048608 | tf_op jit(solution)/shard_map/all_to_all | solution.py:156
  546.3 3.3 all-to-all-start.1
  549.8 17.3 %collective-permute-done = bf16[2,2048,128]{2,1,0:T(8,128)(2,1)S(1)} collective-permute-done((bf16[2,2048,128]{2,1,0:T(8,128)(2,1)S(1)}, bf16[2,2048,128]{2,1,0:T(8,128)(2,1)S(1)}, u32[]{:S(2)}, u32[]{:S(2)}) %collective-permute-start) | collective-permute-done | bytes 1048608 | tf_op jit(solution)/shard_map/ppermute | solution.py:15
  567.3 2.3 collective-permute-start.1
  571.6 21.2 %collective-permute-done.1 = bf16[2,2048,128]{2,1,0:T(8,128)(2,1)} collective-permute-done((bf16[2,2048,128]{2,1,0:T(8,128)(2,1)S(1)}, bf16[2,2048,128]{2,1,0:T(8,128)(2,1)}, u32[]{:S(2)}, u32[]{:S(2)}) %collective-permute-start.1) | collective-permute-done | bytes 1048608 | tf_op jit(solution)/shard_map/ppermute | solution.py:15
  592.9 2.3 collective-permute-start.2
  595.5 2.3 collective-permute-start.6
  597.8 2.8 collective-permute-done.6
  600.6 3.7 collective-permute-start.7
  604.4 36.9 %collective-permute-done.7 = bf16[2,16,1]{1,0,2:T(2,128)(2,1)S(1)} collective-permute-done((bf16[2,16,1]{1,0,2:T(2,128)(2,1)S(1)}, bf16[2,16,1]{1,0,2:T(2,128)(2,1)S(1)}, u32[]{:S(2)}, u32[]{:S(2)}) %collective-permute-start.7) | collective-permute-done | bytes 96 | tf_op jit(solution)/shard_map/ppermute | solution.py:15
  641.3 1.4 collective-permute-start.8
  645.4 21.3 %collective-permute-done.9 = bf16[2,16,1]{1,0,2:T(2,128)(2,1)S(1)} collective-permute-done((bf16[2,16,1]{1,0,2:T(2,128)(2,1)S(1)}, bf16[2,16,1]{1,0,2:T(2,128)(2,1)S(1)}, u32[]{:S(2)}, u32[]{:S(2)}) %collective-permute-start.9) | collective-permute-done | bytes 96 | tf_op jit(solution)/shard_map/ppermute | solution.py:15
  667.8 2.0 collective-permute-start.4
  672.4 1.6 fusion.24
  673.9 19.3 %collective-permute-done.4 = bf16[2,2048,128]{2,1,0:T(8,128)(2,1)S(1)} collective-permute-done((bf16[2,2048,128]{2,1,0:T(8,128)(2,1)S(1)}, bf16[2,2048,128]{2,1,0:T(8,128)(2,1)S(1)}, u32[]{:S(2)}, u32[]{:S(2)}) %collective-permute-start.4) | collective-permute-done | bytes 1048608 | tf_op jit(solution)/shard_map/ppermute | solution.py:15
  693.2 1.7 multiply_bitcast_fusion
  (104 shorter events, 28.4 us)
Async XLA Ops:
  7.2 443.1 %all-gather.3.cloned.1.call-start = ((), (), s32[]{:S(2)}) async-start(), calls=%async_computation.2 | async-start | bytes 25264128 | tf_op jit(solution)/shard_map/all_gather | solution.py:144
  15.4 466.4 %copy-start.5 = (bf16[3,16,5120]{2,1,0:T(8,128)(2,1)S(1)}, bf16[3,16,5120]{2,1,0:T(8,128)(2,1)}, u32[]{:S(2)}) copy-start(bf16[3,16,5120]{2,1,0:T(8,128)(2,1)} %param.14) | copy-start | bytes 1474564
  481.8 11.7 %copy-start.4 = (f32[1024]{0:T(1024)S(1)}, f32[1024]{0:T(1024)}, u32[]{:S(2)}) copy-start(f32[1024]{0:T(1024)} %param.10) | copy-start | bytes 12292
  493.3 1.5 copy-start
  503.6 12.5 %copy-start.3 = (s32[32,16]{0,1:T(8,128)S(1)}, s32[32,16]{0,1:T(8,128)}, u32[]{:S(2)}) copy-start(s32[32,16]{0,1:T(8,128)} %param.11) | copy-start | bytes 6148
  507.3 36.4 %copy-start.2 = (bf16[3,16,640]{2,1,0:T(8,128)(2,1)S(1)}, bf16[3,16,640]{2,1,0:T(8,128)(2,1)}, u32[]{:S(2)}) copy-start(bf16[3,16,640]{2,1,0:T(8,128)(2,1)} %param.15) | copy-start | bytes 184324
  507.3 34.1 %all-to-all-start = ((bf16[2,256,1024]{1,0,2:T(2,128)(2,1)}), bf16[2,256,1024]{1,0,2:T(2,128)(2,1)S(1)}, u32[]{:S(2)}, u32[]{:S(2)}) async-start(bf16[2,256,1024]{1,0,2:T(2,128)(2,1)} %copy.79), calls=%async_computation | async-start | bytes 2097152 | tf_op jit(solution)/shard_map/all_to_all | solution.py:156
  542.3 24.8 %collective-permute-start = (bf16[2,2048,128]{2,1,0:T(8,128)(2,1)S(1)}, bf16[2,2048,128]{2,1,0:T(8,128)(2,1)S(1)}, u32[]{:S(2)}, u32[]{:S(2)}) collective-permute-start(bf16[2,2048,128]{2,1,0:T(8,128)(2,1)S(1)} %bitcast.218), channel_id=1, source_target_pairs={{0,8},{8,0},{16,24},{24,16},{32,40},{40,32},{48,56},{56,48},{64,72... | collective-permute-start | bytes 3145736 | tf_op jit(solution)/shard_map/ppermute | solution.py:15
  546.3 25.0 %all-to-all-start.1 = ((bf16[2,2,8]{1,0,2:T(2,128)(2,1)}), bf16[2,2,8]{1,0,2:T(2,128)(2,1)S(1)}, u32[]{:S(2)}, u32[]{:S(2)}) async-start(bf16[2,2,8]{1,0,2:T(2,128)(2,1)} %copy.82), calls=%async_computation.1 | async-start | bytes 8192 | tf_op jit(solution)/shard_map/all_to_all | solution.py:157
  567.3 25.5 %collective-permute-start.1 = (bf16[2,2048,128]{2,1,0:T(8,128)(2,1)S(1)}, bf16[2,2048,128]{2,1,0:T(8,128)(2,1)}, u32[]{:S(2)}, u32[]{:S(2)}) collective-permute-start(bf16[2,2048,128]{2,1,0:T(8,128)(2,1)S(1)} %broadcast_select_fusion), channel_id=1, source_target_pairs={{0,16},{8,24},{16,0},{24,8},{32,48},{40,56},{48,32},{56,40},{64,80... | collective-permute-start | bytes 3145736 | tf_op jit(solution)/shard_map/ppermute | solution.py:15
  571.6 23.9 %collective-permute-start.5 = (bf16[2,16,1]{1,0,2:T(2,128)(2,1)S(1)}, bf16[2,16,1]{1,0,2:T(2,128)(2,1)S(1)}, u32[]{:S(2)}, u32[]{:S(2)}) collective-permute-start(bf16[2,16,1]{1,0,2:T(2,128)(2,1)S(1)} %all_to_all.33), channel_id=1, source_target_pairs={{0,8},{8,0},{16,24},{24,16},{32,40},{40,32},{48,56},{56,48},{64,72... | collective-permute-start | bytes 200 | tf_op jit(solution)/shard_map/ppermute | solution.py:15
  592.9 49.8 %collective-permute-start.2 = (bf16[2,2048,128]{2,1,0:T(8,128)(2,1)S(1)}, bf16[2,2048,128]{2,1,0:T(8,128)(2,1)S(1)}, u32[]{:S(2)}, u32[]{:S(2)}) collective-permute-start(bf16[2,2048,128]{2,1,0:T(8,128)(2,1)S(1)} %broadcast_select_fusion.1), channel_id=1, source_target_pairs={{0,32},{8,40},{16,48},{24,56},{32,0},{40,8},{48,16},{56,24},{64,96... | collective-permute-start | bytes 3145736 | tf_op jit(solution)/shard_map/ppermute | solution.py:15
  595.5 5.1 collective-permute-start.6
  600.6 40.7 %collective-permute-start.7 = (bf16[2,16,1]{1,0,2:T(2,128)(2,1)S(1)}, bf16[2,16,1]{1,0,2:T(2,128)(2,1)S(1)}, u32[]{:S(2)}, u32[]{:S(2)}) collective-permute-start(bf16[2,16,1]{1,0,2:T(2,128)(2,1)S(1)} %broadcast_select_fusion.6), channel_id=1, source_target_pairs={{0,32},{8,40},{16,48},{24,56},{32,0},{40,8},{48,16},{56,24},{64,96... | collective-permute-start | bytes 200 | tf_op jit(solution)/shard_map/ppermute | solution.py:15
  641.3 3.5 collective-permute-start.8
  642.8 24.8 %collective-permute-start.3 = (bf16[2,2048,128]{2,1,0:T(8,128)(2,1)S(1)}, bf16[2,2048,128]{2,1,0:T(8,128)(2,1)S(1)}, u32[]{:S(2)}, u32[]{:S(2)}) collective-permute-start(bf16[2,2048,128]{2,1,0:T(8,128)(2,1)S(1)} %broadcast_select_fusion.2), channel_id=1, source_target_pairs={{0,64},{8,72},{16,80},{24,88},{32,96},{40,104},{48,112},{56,120},{... | collective-permute-start | bytes 3145736 | tf_op jit(solution)/shard_map/ppermute | solution.py:15
  644.8 21.9 %collective-permute-start.9 = (bf16[2,16,1]{1,0,2:T(2,128)(2,1)S(1)}, bf16[2,16,1]{1,0,2:T(2,128)(2,1)S(1)}, u32[]{:S(2)}, u32[]{:S(2)}) collective-permute-start(bf16[2,16,1]{1,0,2:T(2,128)(2,1)S(1)} %broadcast_select_fusion.8), channel_id=1, source_target_pairs={{0,128},{8,136},{16,144},{24,152},{32,160},{40,168},{48,176},{56,1... | collective-permute-start | bytes 200 | tf_op jit(solution)/shard_map/ppermute | solution.py:15
  667.8 25.4 %collective-permute-start.4 = (bf16[2,2048,128]{2,1,0:T(8,128)(2,1)S(1)}, bf16[2,2048,128]{2,1,0:T(8,128)(2,1)S(1)}, u32[]{:S(2)}, u32[]{:S(2)}) collective-permute-start(bf16[2,2048,128]{2,1,0:T(8,128)(2,1)S(1)} %broadcast_select_fusion.3), channel_id=1, source_target_pairs={{0,128},{8,136},{16,144},{24,152},{32,160},{40,168},{48,176},{56,1... | collective-permute-start | bytes 3145736 | tf_op jit(solution)/shard_map/ppermute | solution.py:15
  669.8 2.3 copy-start.6
  670.7 1.6 copy-start.1
Sparse Core Ops, SparseCore 0:
  9.9 440.3 all-gather.2
where the time goes:
time: 705 us; the launch traced here: 704 us
  waiting for transfers between devices  581 us (82%)
  local copies, waits for them, and re-layouts  50.7 us (7%)
  starting transfers between devices  26.7 us (4%)
  between operations  16.9 us (2%)
  matrix products  16.8 us (2%)
  other arithmetic  11.7 us (2%)
    all_gather x1, waiting for transfers between devices, on_device(): lax.all_gather(key_value_weight, ('dp', 'seq'), axis=0, tiled=True)  435 us
    ppermute x10, waiting for transfers between devices, swapped_2(): lax.ppermute(array, axis, [(i, i ^ 1 << distance) for i in range(lax.axis...  121 us
    unnamed x20, local copies, waits for them, and re-layouts  33 us
    all_to_all x1, waiting for transfers between devices, on_device(): lax.all_to_all(stored_pages, 'seq', split_axis=2, concat_axis=1, tiled=True)  24.3 us
    ppermute x10, starting transfers between devices, swapped_2(): lax.ppermute(array, axis, [(i, i ^ 1 << distance) for i in range(lax.axis...  15.8 us
  transfers between devices with their start and end apart: 13, of which 10 were waited for; matrix products, arithmetic and copies ran while one was open for 3% of the time, Pallas kernels for 0%

commit v1 on v0

v1 whole, which is shorter than its diff:
```python
import math

import jax
import jax.numpy as jnp
from jax import lax
from jax.experimental import pallas as pl
from jax.experimental.pallas import tpu as pltpu
from jax.sharding import PartitionSpec as P

HEADS = 8
HEAD = 128
PAGE = 128
GROUP = 5
MESH = pl.DeviceIdType.MESH
F32 = jnp.float32
BF16 = jnp.bfloat16

WIDTH = 5120
SHARD = 20
PADDED = 32
PAIR_ROWS = 80
BLOCK = 160
TOKENS = 256
CHIP_TOKENS = 512
FRESH = 48
ROWS = CHIP_TOKENS + FRESH
SLAB = CHIP_TOKENS + 16
LANES = 128


def gather_project(
    w_ref,
    prompt_ref,
    decode_ref,
    cos_ref,
    sin_ref,
    live_ref,
    gain_ref,
    pool_ref,
    fresh_ref,
    raw,
    acts,
    weights,
    acc,
    stage,
    squares,
    send_sem,
    recv_sem,
    local_sem,
):
    dp = lax.axis_index("dp")
    seq = lax.axis_index("seq")
    core = lax.rem(seq, 2)
    z_lo = seq // 2
    x = lax.rem(dp, 4)
    z_hi = lax.rem(dp // 4, 2)
    y = dp // 8
    z = z_hi * 4 + z_lo
    pair = z // 2
    odd = lax.rem(z, 2)

    def at(yy, zz, xx, cc):
        return (yy * 8 + (zz // 4) * 4 + xx, lax.rem(zz, 4) * 2 + cc)

    def turn(index, by, size):
        return lax.rem(index + (by + size), size)

    sibling = at(y, z, x, 1 - core)
    inter_z = turn(z, 2 * odd - 1, 8)
    intra_z = z + 1 - 2 * odd
    inter = at(y, inter_z, x, core)
    intra = at(y, intra_z, x, core)
    intra_other = at(y, intra_z, x, 1 - core)
    rights = {"x": at(y, z, turn(x, 1, 4), core), "y": at(turn(y, 1, 4), z, x, core)}
    lefts = {"x": at(y, z, turn(x, -1, 4), core), "y": at(turn(y, -1, 4), z, x, core)}
    far_chips = [jnp.bitwise_xor(z_lo, d) for d in (1, 2, 3)]
    columns = [(dp, chip * 2 + core) for chip in far_chips]

    peers = [
        sibling,
        inter,
        intra,
        intra_other,
        rights["x"],
        lefts["x"],
        rights["y"],
        lefts["y"],
        columns[1],
        columns[2],
    ]
    barrier = pltpu.get_barrier_semaphore()
    for peer in peers:
        pl.semaphore_signal(barrier, inc=1, device_id=peer, device_id_type=MESH)
    pl.semaphore_wait(barrier, len(peers))

    number = [0]
    copies = {}

    def send(key, src, dst, device):
        k = number[0]
        number[0] += 1
        copy = pltpu.make_async_remote_copy(
            src_ref=src,
            dst_ref=dst,
            send_sem=send_sem.at[k],
            recv_sem=recv_sem.at[k],
            device_id=device,
            device_id_type=MESH,
        )
        copy.start()
        copies[key] = copy

    def arrived(*keys):
        for key in keys:
            copies[key].wait_recv()

    slot = odd * 2 + core
    mine = w_ref.at[core]
    other = w_ref.at[1 - core]
    send("w_intra", mine, raw.at[slot], intra)
    send("w_other", other, raw.at[slot], intra_other)
    send("w_sibling", other, raw.at[slot], sibling)

    here = pl.ds(pl.multiple_of(core * TOKENS, TOKENS), TOKENS)
    send("acts", prompt_ref, acts.at[here], sibling)
    own_acts = pltpu.make_async_copy(prompt_ref, acts.at[here], local_sem.at[0])
    own_acts.start()
    own_decode = pltpu.make_async_copy(
        decode_ref, acts.at[pl.ds(CHIP_TOKENS, FRESH)], local_sem.at[1]
    )
    own_decode.start()

    raw[slot] = w_ref[core]
    arrived("w_intra", "w_other", "w_sibling")
    row = lax.broadcasted_iota(jnp.int32, (PAIR_ROWS, 4 * PADDED), 0)
    col = lax.broadcasted_iota(jnp.int32, (PAIR_ROWS, 4 * PADDED), 1)
    inside = jnp.bitwise_and(col, PADDED - 1)
    source = jnp.right_shift(col, 5)
    pick = jnp.where((row == source * SHARD + inside) & (inside < SHARD), 1.0, 0.0).astype(BF16)
    rows = jnp.dot(
        pick, raw[...].reshape(4 * PADDED, 8 * LANES), preferred_element_type=F32
    ).astype(BF16)

    outer = (y, x)
    inner = (x, y)
    inner_axis = ("x", "y")
    outer_axis = ("y", "x")
    for g in range(2):
        for p in range(2):
            for t in range(2):
                tile = g * 4 + p * 2 + t
                weights[g, p, outer[p], pair, inner[p], pl.ds(t * PAIR_ROWS, PAIR_ROWS)] = rows[
                    :, tile * LANES : (tile + 1) * LANES
                ]

    sign = 2 * odd - 1
    blocks = [pair, turn(pair, sign, 4), turn(pair, -sign, 4), turn(pair, 2, 4)]

    def inner_first(g):
        for p in range(2):
            ref = weights.at[g, p, outer[p], pair, inner[p]]
            send(("i1r", g, p), ref, ref, rights[inner_axis[p]])
            send(("i1l", g, p), ref, ref, lefts[inner_axis[p]])

    def inner_second(g):
        for p in range(2):
            arrived(("i1r", g, p), ("i1l", g, p))
            ref = weights.at[g, p, outer[p], pair]
            low = ref.at[turn(inner[p], -1, 4), pl.ds(0, PAIR_ROWS)]
            high = ref.at[turn(inner[p], 1, 4), pl.ds(PAIR_ROWS, PAIR_ROWS)]
            send(("i2r", g, p), low, low, rights[inner_axis[p]])
            send(("i2l", g, p), high, high, lefts[inner_axis[p]])

    def inner_done(g):
        for p in range(2):
            arrived(("i2r", g, p), ("i2l", g, p))

    def z_step(step, g):
        half = (1 - odd) if step == 3 else odd
        for p in range(2):
            if step >= 2:
                arrived(("z", step - 1, g, p))
            ref = weights.at[g, p, outer[p], blocks[step - 1]]
            if step >= 3:
                ref = ref.at[pl.ds(half * 2, 2)]
            send(("z", step, g, p), ref, ref, inter if step % 2 else intra)

    def z_done(g):
        for p in range(2):
            arrived(("z", 4, g, p))

    def outer_first(block, g):
        for p in range(2):
            ref = weights.at[g, p, outer[p], blocks[block]]
            send(("o1r", block, g, p), ref, ref, rights[outer_axis[p]])
            send(("o1l", block, g, p), ref, ref, lefts[outer_axis[p]])

    def outer_second(block, g):
        for p in range(2):
            arrived(("o1r", block, g, p), ("o1l", block, g, p))
            low = weights.at[g, p, turn(outer[p], -1, 4), blocks[block], pl.ds(0, 2)]
            high = weights.at[g, p, turn(outer[p], 1, 4), blocks[block], pl.ds(2, 2)]
            send(("o2r", block, g, p), low, low, rights[outer_axis[p]])
            send(("o2l", block, g, p), high, high, lefts[outer_axis[p]])

    def outer_done(g):
        for block in range(4):
            for p in range(2):
                arrived(("o2r", block, g, p), ("o2l", block, g, p))

    def project(g):
        acc[...] = jnp.zeros_like(acc)

        @pl.loop(0, 4)
        def _(yy):
            left = acts[:, pl.ds(pl.multiple_of(yy * 1280, 1280), 1280)]
            for p in range(2):
                tiles = []
                for t in range(2):
                    pieces = []
                    for zh in range(2):
                        for xx in range(4):
                            for zl in range(2):
                                place = (yy, xx) if p == 0 else (xx, yy)
                                pieces.append(
                                    weights[
                                        g,
                                        p,
                                        place[0],
                                        zh * 2 + zl,
                                        place[1],
                                        pl.ds(t * PAIR_ROWS, PAIR_ROWS),
                                    ]
                                )
                    tiles.append(jnp.concatenate(pieces, axis=0))
                acc[p] += jnp.dot(
                    left, jnp.concatenate(tiles, axis=1), preferred_element_type=F32
                )

    def store_pages(g, head, fields):
        scales = jnp.zeros((16, LANES), F32)
        line = lax.broadcasted_iota(jnp.int32, (16, LANES), 0)
        for page in range(4):
            largest = jnp.max(jnp.abs(fields[page]), axis=(0, 1), keepdims=True)
            scale = ((largest + 1e-06) / 448.0).astype(BF16).astype(F32)
            stage[g, head, pl.ds(page * PAGE, PAGE)] = (fields[page] / scale).astype(BF16)
            scales = jnp.where(line == page, scale, scales)
        stage[g, head, pl.ds(CHIP_TOKENS, 16)] = scales.astype(BF16)

    def all_to_all(g):
        for d in range(3):
            send(
                ("a2a", g, d), stage.at[g, far_chips[d]], pool_ref.at[1 - g, z_lo], columns[d]
            )
        own = pltpu.make_async_copy(
            stage.at[g, z_lo], pool_ref.at[1 - g, z_lo], local_sem.at[2 + g]
        )
        own.start()
        return own

    def values():
        project(0)
        for head in range(4):
            p, lanes = head // 2, pl.ds(head % 2 * LANES, LANES)
            pages = []
            for page in range(4):
                part = pl.ds(page * PAGE, PAGE)
                pages.append(jnp.where(live_ref[part] > 0.5, acc[p, part, lanes], 0.0))
            store_pages(0, head, pages)
        tail = pl.ds(CHIP_TOKENS, FRESH)
        for head in range(4):
            p, lanes = head // 2, pl.ds(head % 2 * LANES, LANES)

            @pl.when(z_lo == head)
            def _():
                fresh_ref[1] = acc[p, tail, lanes].astype(BF16)

    def keys():
        project(1)
        total = jnp.zeros((ROWS, 1), F32)
        for p in range(2):
            total += jnp.sum(acc[p] * acc[p], axis=1, keepdims=True)
        squares[0] = jnp.broadcast_to(total, (ROWS, LANES))
        send("squares", squares.at[0], squares.at[1], sibling)
        arrived("squares")
        squares[1] = lax.rsqrt((squares[0] + squares[1]) * (1.0 / (HEADS * HEAD)) + 1e-06)

        def turned(head, part):
            p, lanes = head // 2, pl.ds(head % 2 * LANES, LANES)
            gain = gain_ref[pl.ds(head * 2 + core, 1), :]
            row = acc[p, part, lanes] * squares[1, part] * gain
            return row * cos_ref[part] + pltpu.roll(row, 64, 1) * sin_ref[part]

        for head in range(4):
            pages = []
            for page in range(4):
                part = pl.ds(page * PAGE, PAGE)
                pages.append(jnp.where(live_ref[part] > 0.5, turned(head, part), 0.0))
            store_pages(1, head, pages)
        tail = pl.ds(CHIP_TOKENS, FRESH)
        for head in range(4):

            @pl.when(z_lo == head)
            def _():
                fresh_ref[0] = turned(head, tail).astype(BF16)

    V, K = 0, 1
    inner_first(V)
    inner_first(K)
    inner_second(V)
    inner_second(K)
    inner_done(V)
    z_step(1, V)
    outer_first(0, V)
    inner_done(K)
    z_step(1, K)
    outer_first(0, K)
    outer_second(0, V)
    outer_second(0, K)
    z_step(2, V)
    outer_first(1, V)
    z_step(2, K)
    outer_first(1, K)
    outer_second(1, V)
    z_step(3, V)
    outer_first(2, V)
    outer_second(1, K)
    z_step(3, K)
    outer_first(2, K)
    outer_second(2, V)
    z_step(4, V)
    z_done(V)
    outer_first(3, V)
    outer_second(2, K)
    z_step(4, K)
    z_done(K)
    outer_first(3, K)
    outer_second(3, V)
    outer_second(3, K)
    own_acts.wait()
    own_decode.wait()
    arrived("acts")
    outer_done(V)
    values()
    own_values = all_to_all(V)
    outer_done(K)
    keys()
    own_keys = all_to_all(K)
    own_values.wait()
    own_keys.wait()
    for g in range(2):
        for d in range(3):
            arrived(("a2a", g, d))
    for copy in copies.values():
        copy.wait_send()


N_COPIES = 4 + 4 * 24 + 1 + 6


def attend_expand(place_ref, q_ref, near_ref, far_ref, fresh_ref, out_ref, fork_ref, weight):
    factor = 1.0 / math.sqrt(HEAD)
    steps = 3
    rows = GROUP * steps * 8
    lane = lax.broadcasted_iota(jnp.int32, (1, LANES), 1)
    r = lax.broadcasted_iota(jnp.int32, (rows, steps * 8), 0)
    c = lax.broadcasted_iota(jnp.int32, (rows, steps * 8), 1)
    visible = (jnp.bitwise_and(r, 7) == jnp.bitwise_and(c, 7)) & (
        jnp.right_shift(lax.rem(r, steps * 8), 3) >= jnp.right_shift(c, 3)
    )
    results = []
    for side, pool in enumerate((near_ref, far_ref)):
        samples = slice(side * 8, side * 8 + 8)
        query = jnp.concatenate(
            [
                q_ref[:, samples, g * HEAD : (g + 1) * HEAD].astype(F32).reshape(steps * 8, HEAD)
                for g in range(GROUP)
            ],
            axis=0,
        ).astype(BF16)
        new = [
            fresh_ref[kind]
            .astype(F32)
            .reshape(steps, 16, HEAD)[:, samples]
            .reshape(steps * 8, HEAD)
            .astype(BF16)
            for kind in range(2)
        ]
        length = place_ref[side, 16]
        sums = jnp.zeros((rows, LANES), F32)
        for page in range(16):
            chip, part = page // 4, page % 4
            keys = pool[0, chip, part * PAGE : (part + 1) * PAGE]
            scale = pool[0, chip, CHIP_TOKENS : CHIP_TOKENS + 16].astype(F32)[part : part + 1]
            raw = lax.dot_general(
                query, keys, (((1,), (1,)), ((), ())), preferred_element_type=F32
            )
            live = place_ref[side, page] * PAGE + lane < length
            cached = jnp.where(live, jnp.exp(raw * scale * factor), 0.0)
            weight[:, page * PAGE : (page + 1) * PAGE] = cached
            sums += cached
        fresh_raw = lax.dot_general(
            query, new[0], (((1,), (1,)), ((), ())), preferred_element_type=F32
        )
        fresh = jnp.where(visible, jnp.exp(fresh_raw * factor), 0.0)
        total = jnp.sum(sums, axis=1, keepdims=True) + jnp.sum(fresh, axis=1, keepdims=True)
        result = jnp.dot(
            (fresh / total).astype(BF16), new[1], preferred_element_type=F32
        )
        for page in range(16):
            chip, part = page // 4, page % 4
            scale = pool[1, chip, CHIP_TOKENS : CHIP_TOKENS + 16].astype(F32)[part : part + 1]
            portion = weight[:, page * PAGE : (page + 1) * PAGE] / total * scale
            result += jnp.dot(
                portion.astype(BF16),
                pool[1, chip, part * PAGE : (part + 1) * PAGE],
                preferred_element_type=F32,
            )
        results.append(result)
    for g in range(GROUP):
        span = slice(g * steps * 8, (g + 1) * steps * 8)
        both = jnp.concatenate(
            [piece[span].reshape(steps, 8, HEAD) for piece in results], axis=1
        )
        out_ref[:, :, g * HEAD : (g + 1) * HEAD] = both.astype(BF16)
    for kind in range(2):
        for page in range(16):
            chip, part = page // 4, page % 4
            scale = far_ref[kind, chip, CHIP_TOKENS : CHIP_TOKENS + 16].astype(F32)[
                part : part + 1
            ]
            fork_ref[0, kind, page * PAGE : (page + 1) * PAGE] = (
                far_ref[kind, chip, part * PAGE : (part + 1) * PAGE].astype(F32) * scale
            )


def on_device(
    prompt_hidden,
    key_value_weight,
    key_norm_gain,
    page_table,
    lengths,
    source_replica,
    decode_hidden,
    queries,
):
    steps, paired, width = queries.shape
    seq_at = lax.axis_index("seq")
    replica = lax.axis_index("dp")
    replicas = lax.axis_size("dp")
    partner = source_replica[replica]
    own_length = lengths[replica]
    far_length = lengths[partner]

    split = key_value_weight.reshape(SHARD, 2, 4, 2, HEAD)[:, ::-1]
    split = split.transpose(3, 0, 1, 2, 4).reshape(2, SHARD, 8 * HEAD)
    split = jnp.pad(split, ((0, 0), (0, PADDED - SHARD), (0, 0)))

    pages = lax.dynamic_slice(page_table, (replica, seq_at // 2 * 4), (1, 4))[0]
    places = (pages[:, None] * PAGE + jnp.arange(PAGE, dtype=jnp.int32)).reshape(-1)
    starts = jnp.where(jnp.arange(paired) < paired // 2, own_length, far_length)
    new_places = (starts[None, :] + jnp.arange(steps, dtype=jnp.int32)[:, None]).reshape(-1)
    half = HEAD // 2
    freq = 500000.0 ** (-jnp.arange(half, dtype=F32) * 2.0 / HEAD)
    angle = jnp.concatenate([places, new_places]).astype(F32)[:, None] * freq
    cosine, sine = jnp.cos(angle), jnp.sin(angle)
    cosine = jnp.concatenate([cosine, cosine], axis=1)
    sine = jnp.concatenate([-sine, sine], axis=1)
    live = jnp.broadcast_to((places < own_length)[:, None], (CHIP_TOKENS, LANES)).astype(F32)

    vmem = pl.BlockSpec(memory_space=pltpu.VMEM)
    hbm = pl.BlockSpec(memory_space=pl.ANY)
    pool, fresh = pl.pallas_call(
        gather_project,
        out_shape=(
            jax.ShapeDtypeStruct((2, 4, SLAB, LANES), BF16),
            jax.ShapeDtypeStruct((2, FRESH, LANES), BF16),
        ),
        in_specs=[vmem, hbm, hbm, vmem, vmem, vmem, vmem],
        out_specs=(hbm, vmem),
        scratch_shapes=[
            pltpu.VMEM((4, PADDED, 8 * LANES), BF16),
            pltpu.VMEM((ROWS, WIDTH), BF16),
            pltpu.VMEM((2, 2, 4, 4, 4, BLOCK, LANES), BF16),
            pltpu.VMEM((2, ROWS, 2 * LANES), F32),
            pltpu.VMEM((2, 4, SLAB, LANES), BF16),
            pltpu.VMEM((2, ROWS, LANES), F32),
            pltpu.SemaphoreType.DMA((N_COPIES,)),
            pltpu.SemaphoreType.DMA((N_COPIES,)),
            pltpu.SemaphoreType.DMA((4,)),
        ],
        compiler_params=pltpu.CompilerParams(
            collective_id=0, has_side_effects=True, vmem_limit_bytes=44 * 1024 * 1024
        ),
    )(
        split,
        prompt_hidden[0],
        decode_hidden.reshape(steps * paired, WIDTH),
        cosine,
        sine,
        live,
        key_norm_gain.reshape(HEADS, HEAD),
    )

    def swap(mask):
        def branch(array):
            return lax.ppermute(array, "dp", [(i, i ^ mask) for i in range(replicas)])

        return branch

    mask = jnp.bitwise_xor(partner, replica)
    far_pool = lax.switch(mask - 1, [swap(m) for m in range(1, replicas)], pool)

    table = jnp.stack([page_table[replica], page_table[partner]])
    place = jnp.concatenate([table, jnp.stack([own_length, far_length])[:, None]], axis=1)
    smem = pl.BlockSpec(memory_space=pltpu.SMEM)
    attended, forked = pl.pallas_call(
        attend_expand,
        out_shape=(
            jax.ShapeDtypeStruct((steps, paired, width), BF16),
            jax.ShapeDtypeStruct((1, 2, 2048, LANES), F32),
        ),
        in_specs=[smem, vmem, vmem, vmem, vmem],
        out_specs=(vmem, vmem),
        scratch_shapes=[pltpu.VMEM((GROUP * steps * 8, 2048), F32)],
        compiler_params=pltpu.CompilerParams(vmem_limit_bytes=32 * 1024 * 1024),
    )(place, queries, pool, far_pool, fresh)
    return attended, forked


def solution(mesh):
    return jax.shard_map(
        on_device,
        mesh=mesh,
        in_specs=(
            P("dp", "seq", None),
            P(("dp", "seq"), None),
            P(),
            P(),
            P(),
            P(),
            P(None, "dp", None),
            P(None, "dp", "seq"),
        ),
        out_specs=(P(None, "dp", "seq"), P("dp", None, None, "seq")),
        check_vma=False,
    )
```

time: 705 us -> 166 us (0.24)
  the two profiles are of different devices: /device:TPU:6 before, /device:TPU:33 now
where the time goes in v1:
time: 166 us; the launch traced here: 165 us
  Pallas kernels  94.5 us (57%)
  waiting for transfers between devices  51.9 us (31%)
  other arithmetic  5.73 us (3%)
  local copies, waits for them, and re-layouts  5.3 us (3%)
  starting transfers between devices  4.17 us (3%)
  between operations  3.36 us (2%)
    pallas_call x1, Pallas kernels, on_device(): pl.pallas_call(gather_project, out_shape=(jax.ShapeDtypeStruct((2, 4, SLA...  90.1 us
    ppermute x1, waiting for transfers between devices, branch(): return lax.ppermute(array, 'dp', [(i, i ^ mask) for i in range(replicas)])  51.9 us
    pallas_call x1, Pallas kernels, on_device(): pl.pallas_call(attend_expand, out_shape=(jax.ShapeDtypeStruct((steps, pai...  4.45 us
    ppermute x1, starting transfers between devices, branch(): return lax.ppermute(array, 'dp', [(i, i ^ mask) for i in range(replicas)])  4.17 us
  transfers between devices with their start and end apart: 1, of which 1 were waited for; matrix products, arithmetic and copies ran while one was open for 0% of the time, Pallas kernels for 0%

profile of v1, /device:TPU:33, one launch (start us, length us, event | category | flops | bytes accessed | tf_op | source)
XLA Modules:
  0.0 165.2 jit_solution(784859504466397790)
XLA Ops:
  0.6 0.9 multiply_reduce_fusion
  1.5 1.2 dynamic_slice.19
  5.4 1.3 fusion.1
  6.7 1.3 compare_select_fusion
  8.0 1.4 add_bitcast_fusion.1
  9.4 0.1 copy.16
  9.5 0.1 add.69
  9.6 0.7 compare_convert_fusion
  10.3 0.1 add_bitcast_fusion
  10.4 0.8 constant_dynamic-slice_fusion.1
  11.2 0.1 copy.19
  11.3 0.1 copy.20
  11.4 0.1 pad_add_fusion.place_ref
  11.4 0.9 reshape.73
  12.4 0.0 copy-start.1
  12.5 0.1 broadcast_in_dim.25.live_ref
  12.7 1.1 fusion
  13.8 0.2 pad_maximum_fusion
  14.0 0.4 copy-done
  14.4 90.1 %shard_map.95 = (bf16[2,4,528,128]{3,2,1,0:T(8,128)(2,1)S(1)}, bf16[2,48,128]{2,1,0:T(8,128)(2,1)S(1)}) custom-call(bf16[2,32,1024]{2,1,0:T(8,128)(2,1)S(1)} %pad.4.w_ref, bf16[256,5120]{1,0:T(8,128)(2,1)S(1)} %bitcast.16, bf16[48,5120]{1,0:T(8,128)(2,1)S(1)} %bitcast.17, f32[560,128]{1,0:T(8,128)S(1)} %get-tuple-element.76.cos_ref, ...), custom_call_target="tpu_custom_call" | custom-call | tf_op jit(solution)/shard_map/pallas_call | solution.py:473
  104.4 56.2 %conditional.1 = (bf16[2,4,528,128]{3,2,1,0:T(8,128)(2,1)}) conditional(s32[]{:T(128)} %clamp.3, bf16[2,4,528,128]{3,2,1,0:T(8,128)(2,1)S(1)} %get-tuple-element.67.near_ref, bf16[2,4,528,128]{3,2,1,0:T(8,128)(2,1)S(1)} %get-tuple-element.67.near_ref, ...), branch_computations={%region_0.1_spmd, %region_1.2_spmd, %region_2.3_spmd, %region_3.4_... | conditional | bytes 4325424 | solution.py:512
  104.7 4.2 %collective-permute-start.29 = (bf16[2,4,528,128]{3,2,1,0:T(8,128)(2,1)S(1)}, bf16[2,4,528,128]{3,2,1,0:T(8,128)(2,1)}, u32[]{:S(2)}, u32[]{:S(2)}) collective-permute-start(bf16[2,4,528,128]{3,2,1,0:T(8,128)(2,1)S(1)} %param.29), channel_id=1, source_target_pairs={{0,240},{8,248},{16,224},{24,232},{32,208},{40,216},{48,192},{56,2... | collective-permute-start | bytes 3244040 | tf_op jit(solution)/shard_map/cond/branch_29_fun/ppermute | solution.py:507
  108.8 51.9 %collective-permute-done.29 = bf16[2,4,528,128]{3,2,1,0:T(8,128)(2,1)} collective-permute-done((bf16[2,4,528,128]{3,2,1,0:T(8,128)(2,1)S(1)}, bf16[2,4,528,128]{3,2,1,0:T(8,128)(2,1)}, u32[]{:S(2)}, u32[]{:S(2)}) %collective-permute-start.29) | collective-permute-done | bytes 1081376 | tf_op jit(solution)/shard_map/cond/branch_29_fun/ppermute | solution.py:507
  160.7 4.5 %shard_map.96 = (bf16[3,16,640]{2,1,0:T(8,128)(2,1)}, f32[1,2,2048,128]{3,2,1,0:T(8,128)}) custom-call(s32[2,17]{1,0:T(2,128)S(1)} %pad_add_fusion.place_ref, bf16[3,16,640]{2,1,0:T(8,128)(2,1)S(1)} %copy-done.2, bf16[2,4,528,128]{3,2,1,0:T(8,128)(2,1)S(1)} %get-tuple-element.67.near_ref, bf16[2,4,528,128]{3,2,1,0:T(8,128)(2,1)} %get-tuple-element.78.far_ref, ...), custom_call_target="tpu_custom_call" | custom-call | tf_op jit(solution)/shard_map/pallas_call | solution.py:517
  (14 shorter events, 0.2 us)
Async XLA Ops:
  12.4 1.6 copy-start.1
  12.5 1.9 %copy-start = (bf16[1,256,5120]{2,1,0:T(8,128)(2,1)S(1)}, bf16[1,256,5120]{2,1,0:T(8,128)(2,1)}, u32[]{:S(2)}) copy-start(bf16[1,256,5120]{2,1,0:T(8,128)(2,1)} %param.39) | copy-start | bytes 7864324
  12.7 1.7 %copy-start.3 = (f32[1024]{0:T(1024)S(1)}, f32[1024]{0:T(1024)}, u32[]{:S(2)}) copy-start(f32[1024]{0:T(1024)} %param.41) | copy-start | bytes 12292
  14.4 146.3 %copy-start.2 = (bf16[3,16,640]{2,1,0:T(8,128)(2,1)S(1)}, bf16[3,16,640]{2,1,0:T(8,128)(2,1)}, u32[]{:S(2)}) copy-start(bf16[3,16,640]{2,1,0:T(8,128)(2,1)} %q_ref.1) | copy-start | bytes 184324
  104.7 56.0 %collective-permute-start.29 = (bf16[2,4,528,128]{3,2,1,0:T(8,128)(2,1)S(1)}, bf16[2,4,528,128]{3,2,1,0:T(8,128)(2,1)}, u32[]{:S(2)}, u32[]{:S(2)}) collective-permute-start(bf16[2,4,528,128]{3,2,1,0:T(8,128)(2,1)S(1)} %param.29), channel_id=1, source_target_pairs={{0,240},{8,248},{16,224},{24,232},{32,208},{40,216},{48,192},{56,2... | collective-permute-start | bytes 3244040 | tf_op jit(solution)/shard_map/cond/branch_29_fun/ppermute | solution.py:507
